TPU v7x, 32 devices: a whole 2x2x4 slice. The times are simulated.
32 devices in a mesh: wide: 16 (over z, x, core), narrow: 2 (over y).
Axes of the slice: x: 2, y: 2, z: 4, core: 2. Of those that a mesh axis runs over, the one named last changes fastest.
Arguments:
- tokens: bfloat16 [32, 1024, 768], P(('wide', 'narrow')), may hold values from -6 to 6
- lengths: int32 [32, 4], P(('wide', 'narrow')), may hold values from 1 to 512, 1024 in all within a row
- cotangent: bfloat16 [32, 1024, 768], P(('wide', 'narrow')), may hold values from -6 to 6
- vectors: bfloat16 [11, 768], P(None, ('wide', 'narrow')), may hold values from -6 to 3, as said below
- time_recept: bfloat16 [589824], P(('wide', 'narrow')), may hold values from -0.21875 to 0.21875
- time_key: bfloat16 [589824], P(('wide', 'narrow')), may hold values from -0.21875 to 0.21875
- time_value: bfloat16 [589824], P(('wide', 'narrow')), may hold values from -0.21875 to 0.21875
- time_output: bfloat16 [589824], P(('wide', 'narrow')), may hold values from -1.25 to 1.25
- channel_key: bfloat16 [2359296], P(('wide', 'narrow')), may hold values from -0.21875 to 0.21875
- channel_value: bfloat16 [2359296], P(('wide', 'narrow')), may hold values from -0.109375 to 0.109375
- channel_recept: bfloat16 [589824], P(('wide', 'narrow')), may hold values from -0.21875 to 0.21875
Outputs:
- result: bfloat16 [32, 1024, 768], P(('wide', 'narrow'))
- input_grad: bfloat16 [32, 1024, 768], P(('wide', 'narrow'))
- vectors_grad: float32 [11, 768], P(None, ('wide', 'narrow'))
- time_recept_grad: float32 [589824], P(('wide', 'narrow'))
- time_key_grad: float32 [589824], P(('wide', 'narrow'))
- time_value_grad: float32 [589824], P(('wide', 'narrow'))
- time_output_grad: float32 [589824], P(('wide', 'narrow'))
- channel_key_grad: float32 [2359296], P(('wide', 'narrow'))
- channel_value_grad: float32 [2359296], P(('wide', 'narrow'))
- channel_recept_grad: float32 [589824], P(('wide', 'narrow'))
Inputs may be any that keep to these rules, and one draw needn't show every extreme that they name: Each row's 4 document lengths sum to 1024; each row's longest document has 512 tokens. `vectors`: the gains lie in [0.5, 1.5], the biases in [-0.5, 0.5], the five mix rows in [0, 1], decay in [-6, 3] and bonus in [-1.5, 1.5].
All inputs are finite; a program needn't handle non-finite values.
Results may differ from a plain program's by a relative error of at most 0.0085.
Values may be sent and summed in bfloat16 or wider, within the bound.
A program may use at most 256 MiB of HBM per device.

v0:
```python
from functools import partial

import jax
import jax.numpy as jnp
from jax import lax
from jax.sharding import PartitionSpec as P

BLOCK = 32


epsilon = 1e-05


def layer_norm(signal, gain_vec, offset):
    centred = signal - jnp.mean(signal, axis=-1, keepdims=True)
    spread = jnp.mean(centred * centred, axis=-1, keepdims=True)
    return centred * lax.rsqrt(spread + epsilon) * gain_vec + offset


def continue_mask(lengths, length):
    offsets = jnp.cumsum(lengths, axis=-1) - lengths
    positions = jnp.arange(length, dtype=jnp.int32)
    matches = (positions[None, :, None] == offsets[:, None, :]).astype(jnp.float32)
    return 1.0 - jnp.sum(matches, axis=-1)


def shifted(signal, text_persists):
    earlier = jnp.concatenate([jnp.zeros_like(signal[:, :1]), signal[:, :-1]], axis=1)
    return earlier * text_persists[..., None]


def mixing(normed, before, mix_ratio):
    return mix_ratio * normed + (1.0 - mix_ratio) * before


def front_time(signal, gain_vec, offset, ratio_recept, ratio_key, ratio_value, text_persists):
    normed = layer_norm(signal, gain_vec, offset)
    before = shifted(normed, text_persists)
    return (
        mixing(normed, before, ratio_recept),
        mixing(normed, before, ratio_key),
        mixing(normed, before, ratio_value),
    )


def front_channel(signal, gain_vec, offset, ratio_channel, ratio_gate, text_persists):
    normed = layer_norm(signal, gain_vec, offset)
    before = shifted(normed, text_persists)
    return (mixing(normed, before, ratio_channel), mixing(normed, before, ratio_gate))


def block_weighted_kv_sum(
    address_unmixed, content_unmixed, text_persists, fading_speed, initial_extra_share
):
    row_count, length, model_width = address_unmixed.shape
    block_size = min(BLOCK, length)
    block_count = length // block_size
    position = jnp.arange(block_size, dtype=jnp.float32)
    spacing = position[:, None] - 1.0 - position[None, :]
    earlier = position[None, :] < position[:, None]
    pair_decay = jnp.exp(jnp.minimum(spacing[:, :, None] * fading_speed, 0.0))
    rising = jnp.exp(position[:, None] * fading_speed)
    trailing = jnp.exp((block_size - 1.0 - position)[:, None] * fading_speed)
    stretch = jnp.exp(block_size * fading_speed)

    def arrange(tensor_in):
        split = tensor_in.reshape((row_count, block_count, block_size) + tensor_in.shape[2:])
        return jnp.swapaxes(split, 0, 1)

    def advance(carry_state, pieces):
        upper_running_state, lower_running_state = carry_state
        tile_address_rows, tile_content_rows, continue_block = pieces
        segment = jnp.cumsum(1.0 - continue_block, axis=-1)
        same = earlier[None] & (segment[:, :, None] == segment[:, None, :])
        pair = jnp.where(same[..., None], pair_decay[None], 0.0)
        weight = jnp.exp(tile_address_rows)
        upper_inner_sum = jnp.einsum(
            "rijd,rjd->rid", pair, weight * tile_content_rows, precision=lax.Precision.HIGHEST
        )
        lower_inner_sum = jnp.einsum("rijd,rjd->rid", pair, weight, precision=lax.Precision.HIGHEST)
        carried = jnp.where(segment == 0.0, 1.0, 0.0)
        entering_scale = rising[None] * carried[..., None]
        present_extra_factor = jnp.exp(initial_extra_share + tile_address_rows)
        running_numerator = (
            upper_inner_sum
            + entering_scale * upper_running_state[:, None, :]
            + present_extra_factor * tile_content_rows
        )
        running_denominator = (
            lower_inner_sum
            + entering_scale * lower_running_state[:, None, :]
            + present_extra_factor
        )
        ending = jnp.where(segment == segment[:, -1:], 1.0, 0.0)
        settled = ending[..., None] * weight * trailing[None]
        factor = carried[:, -1:] * stretch
        next_top = factor * upper_running_state + jnp.sum(settled * tile_content_rows, axis=1)
        next_bottom = factor * lower_running_state + jnp.sum(settled, axis=1)
        return ((next_top, next_bottom), running_numerator / running_denominator)

    zero_state = jnp.zeros((row_count, model_width), jnp.float32)
    _, outputs = lax.scan(
        jax.checkpoint(advance),
        (zero_state, zero_state),
        (arrange(address_unmixed), arrange(content_unmixed), arrange(text_persists)),
    )
    return jnp.swapaxes(outputs, 0, 1).reshape(row_count, length, model_width)


def temporal_gate(
    receptance_before_mixing,
    address_unmixed,
    content_unmixed,
    decay_parameter,
    initial_extra_share,
    text_persists,
):
    blended_state = block_weighted_kv_sum(
        address_unmixed,
        content_unmixed,
        text_persists,
        -jnp.exp(decay_parameter),
        initial_extra_share,
    )
    return jax.nn.sigmoid(receptance_before_mixing) * blended_state


def multiply(left_in, right_in):
    return jnp.dot(left_in, right_in, preferred_element_type=jnp.float32)


def outer_sum(left_in, right_in):
    return jnp.einsum("nd,ne->de", left_in, right_in, preferred_element_type=jnp.float32)


def back_product(grad_in, matrix):
    return jnp.einsum("ne,de->nd", grad_in, matrix, preferred_element_type=jnp.float32)


def per_device(
    tokens,
    lengths,
    cotangent,
    vectors,
    time_recept,
    time_key,
    time_value,
    time_output,
    channel_key,
    channel_value,
    channel_recept,
):
    row_count, length, model_width = tokens.shape
    token_count = row_count * length
    shape_three = (row_count, length, model_width)
    gathered = (
        lax.all_gather(vectors, ("wide", "narrow"), axis=1, tiled=True),
        lax.all_gather(time_recept, ("wide", "narrow"), axis=0, tiled=True),
        lax.all_gather(time_key, ("wide", "narrow"), axis=0, tiled=True),
        lax.all_gather(time_value, ("wide", "narrow"), axis=0, tiled=True),
        lax.all_gather(time_output, ("wide", "narrow"), axis=0, tiled=True),
        lax.all_gather(channel_key, ("wide", "narrow"), axis=0, tiled=True),
        lax.all_gather(channel_value, ("wide", "narrow"), axis=0, tiled=True),
        lax.all_gather(channel_recept, ("wide", "narrow"), axis=0, tiled=True),
    )
    all_params, all_recept, all_key, all_value, all_output, all_expand, all_shrink, all_gate = (
        gathered
    )
    hidden_width = all_expand.shape[0] // model_width
    params = all_params.astype(jnp.float32)
    recept_mat = all_recept.reshape(model_width, model_width)
    key_mat = all_key.reshape(model_width, model_width)
    value_mat = all_value.reshape(model_width, model_width)
    output_mat = all_output.reshape(model_width, model_width)
    expand_mat = all_expand.reshape(model_width, hidden_width)
    shrink_mat = all_shrink.reshape(hidden_width, model_width)
    gate_mat = all_gate.reshape(model_width, model_width)
    text_persists = continue_mask(lengths, length)
    inputs = tokens.astype(jnp.float32)
    (mixed_recept, mixed_key, mixed_value), pull_front = jax.vjp(
        partial(front_time, text_persists=text_persists),
        inputs,
        params[0],
        params[1],
        params[2],
        params[3],
        params[4],
    )
    low_recept = mixed_recept.astype(jnp.bfloat16).reshape(token_count, model_width)
    low_key = mixed_key.astype(jnp.bfloat16).reshape(token_count, model_width)
    low_value = mixed_value.astype(jnp.bfloat16).reshape(token_count, model_width)
    receptance_before_mixing = multiply(low_recept, recept_mat).reshape(shape_three)
    address_unmixed = multiply(low_key, key_mat).reshape(shape_three)
    content_unmixed = multiply(low_value, value_mat).reshape(shape_three)
    attended, gate_pullback = jax.vjp(
        partial(temporal_gate, text_persists=text_persists),
        receptance_before_mixing,
        address_unmixed,
        content_unmixed,
        params[5],
        params[6],
    )
    low_attend = attended.astype(jnp.bfloat16).reshape(token_count, model_width)
    middle = inputs + multiply(low_attend, output_mat).reshape(shape_three)
    (channel_in, gate_in), pull_channel = jax.vjp(
        partial(front_channel, text_persists=text_persists),
        middle,
        params[7],
        params[8],
        params[9],
        params[10],
    )
    low_channel = channel_in.astype(jnp.bfloat16).reshape(token_count, model_width)
    low_gatein = gate_in.astype(jnp.bfloat16).reshape(token_count, model_width)
    expanded = multiply(low_channel, expand_mat)
    squared = jnp.square(jnp.maximum(expanded, 0.0)).astype(jnp.bfloat16)
    shrunk = multiply(squared, shrink_mat)
    gate_value = jax.nn.sigmoid(multiply(low_gatein, gate_mat))
    result = middle + (gate_value * shrunk).reshape(shape_three)
    back_recept, back_key, back_value, back_output, back_expand, back_shrink, back_gate = (
        lax.all_gather(time_recept, ("wide", "narrow"), axis=0, tiled=True),
        lax.all_gather(time_key, ("wide", "narrow"), axis=0, tiled=True),
        lax.all_gather(time_value, ("wide", "narrow"), axis=0, tiled=True),
        lax.all_gather(time_output, ("wide", "narrow"), axis=0, tiled=True),
        lax.all_gather(channel_key, ("wide", "narrow"), axis=0, tiled=True),
        lax.all_gather(channel_value, ("wide", "narrow"), axis=0, tiled=True),
        lax.all_gather(channel_recept, ("wide", "narrow"), axis=0, tiled=True),
    )
    recept_back = back_recept.reshape(model_width, model_width)
    key_back = back_key.reshape(model_width, model_width)
    value_back = back_value.reshape(model_width, model_width)
    output_back = back_output.reshape(model_width, model_width)
    expand_back = back_expand.reshape(model_width, hidden_width)
    shrink_back = back_shrink.reshape(hidden_width, model_width)
    gate_back = back_gate.reshape(model_width, model_width)
    upstream = cotangent.astype(jnp.float32).reshape(token_count, model_width)
    grad_shrunk = (upstream * gate_value).astype(jnp.bfloat16)
    grad_gate = (upstream * shrunk * gate_value * (1.0 - gate_value)).astype(jnp.bfloat16)
    shrink_grad = outer_sum(squared, grad_shrunk)
    gate_grad = outer_sum(low_gatein, grad_gate)
    grad_squared = back_product(grad_shrunk, shrink_back)
    grad_expanded = (grad_squared * 2.0 * jnp.maximum(expanded, 0.0)).astype(jnp.bfloat16)
    expand_grad = outer_sum(low_channel, grad_expanded)
    grad_channel_in = back_product(grad_expanded, expand_back).reshape(shape_three)
    grad_gate_in = back_product(grad_gate, gate_back).reshape(shape_three)
    grad_norm_mid, grad_gain_two, grad_bias_two, grad_mix_channel, grad_mix_gate = pull_channel(
        (grad_channel_in, grad_gate_in)
    )
    grad_middle = grad_norm_mid + upstream.reshape(shape_three)
    grad_attend = grad_middle.reshape(token_count, model_width).astype(jnp.bfloat16)
    output_grad = outer_sum(low_attend, grad_attend)
    attended_gradient = back_product(grad_attend, output_back).reshape(shape_three)
    acceptance_grad, address_grad, content_grad, fading_grad, extra_reward_grad = gate_pullback(
        attended_gradient
    )
    low_grad_recept = acceptance_grad.reshape(token_count, model_width).astype(jnp.bfloat16)
    low_grad_key = address_grad.reshape(token_count, model_width).astype(jnp.bfloat16)
    low_grad_value = content_grad.reshape(token_count, model_width).astype(jnp.bfloat16)
    recept_grad = outer_sum(low_recept, low_grad_recept)
    key_grad = outer_sum(low_key, low_grad_key)
    value_grad = outer_sum(low_value, low_grad_value)
    grad_mixed_recept = back_product(low_grad_recept, recept_back).reshape(shape_three)
    grad_mixed_key = back_product(low_grad_key, key_back).reshape(shape_three)
    grad_mixed_value = back_product(low_grad_value, value_back).reshape(shape_three)
    grad_norm_in, grad_gain_one, grad_bias_one, grad_mix_recept, grad_mix_key, grad_mix_value = (
        pull_front((grad_mixed_recept, grad_mixed_key, grad_mixed_value))
    )
    input_grad = (grad_middle + grad_norm_in).astype(jnp.bfloat16)
    vectors_grad = jnp.stack(
        [
            grad_gain_one,
            grad_bias_one,
            grad_mix_recept,
            grad_mix_key,
            grad_mix_value,
            fading_grad,
            extra_reward_grad,
            grad_gain_two,
            grad_bias_two,
            grad_mix_channel,
            grad_mix_gate,
        ]
    )
    recept_flat = recept_grad.reshape(-1)
    key_flat = key_grad.reshape(-1)
    value_flat = value_grad.reshape(-1)
    output_flat = output_grad.reshape(-1)
    expand_flat = expand_grad.reshape(-1)
    shrink_flat = shrink_grad.reshape(-1)
    gate_flat = gate_grad.reshape(-1)
    summed = (
        lax.psum_scatter(vectors_grad, ("wide", "narrow"), scatter_dimension=1, tiled=True),
        lax.psum_scatter(recept_flat, ("wide", "narrow"), scatter_dimension=0, tiled=True),
        lax.psum_scatter(key_flat, ("wide", "narrow"), scatter_dimension=0, tiled=True),
        lax.psum_scatter(value_flat, ("wide", "narrow"), scatter_dimension=0, tiled=True),
        lax.psum_scatter(output_flat, ("wide", "narrow"), scatter_dimension=0, tiled=True),
        lax.psum_scatter(expand_flat, ("wide", "narrow"), scatter_dimension=0, tiled=True),
        lax.psum_scatter(shrink_flat, ("wide", "narrow"), scatter_dimension=0, tiled=True),
        lax.psum_scatter(gate_flat, ("wide", "narrow"), scatter_dimension=0, tiled=True),
    )
    sum_params, sum_recept, sum_key, sum_value, sum_output, sum_expand, sum_shrink, sum_gate = (
        summed
    )
    return (
        result.astype(jnp.bfloat16),
        input_grad,
        sum_params,
        sum_recept,
        sum_key,
        sum_value,
        sum_output,
        sum_expand,
        sum_shrink,
        sum_gate,
    )


def solution(mesh):
    placed = (
        P(("wide", "narrow"), None, None),
        P(("wide", "narrow"), None),
        P(("wide", "narrow"), None, None),
        P(None, ("wide", "narrow")),
        P(("wide", "narrow")),
        P(("wide", "narrow")),
        P(("wide", "narrow")),
        P(("wide", "narrow")),
        P(("wide", "narrow")),
        P(("wide", "narrow")),
        P(("wide", "narrow")),
    )
    return jax.shard_map(
        per_device,
        mesh=mesh,
        in_specs=placed,
        out_specs=(
            P(("wide", "narrow"), None, None),
            P(("wide", "narrow"), None, None),
            P(None, ("wide", "narrow")),
            P(("wide", "narrow")),
            P(("wide", "narrow")),
            P(("wide", "narrow")),
            P(("wide", "narrow")),
            P(("wide", "narrow")),
            P(("wide", "narrow")),
            P(("wide", "narrow")),
        ),
        check_vma=False,
    )
```

profile of v0, /device:TPU:0, one launch (start us, length us, event | category | flops | bytes accessed | tf_op | source)
XLA Modules:
  0.0 1793.8 jit_solution(11828592368988375443)
XLA Ops:
  14.0 70.7 %all-gather = bf16[32,24,11]{1,2,0:T(8,128)(2,1)S(1)} all-gather(bf16[1,24,11]{1,2,0:T(8,128)(2,1)} %bitcast.529), channel_id=1, replica_groups=mesh['wide'=16,'narrow'=2] {'wide','narrow'}, dimensions={0}, use_global_device_ids=true | all-gather | bytes 17424 | tf_op jit(solution)/shard_map/all_gather | solution.py:157
  90.9 4.0 add_convert_fusion.3
  97.4 4.4 convolution_bitcast_fusion.2
  101.9 22.0 %all-gather.13.cloned.1.call-done = bf16[589824]{0:T(1024)(128)(2,1)} async-done(((bf16[18432]{0:T(1024)(128)(2,1)}), bf16[589824]{0:T(1024)(128)(2,1)}) %all-gather.13.cloned.1.call-update) | async-done | bytes 1179664 | tf_op jit(solution)/shard_map/all_gather | solution.py:160
  127.2 5.0 convolution_bitcast_fusion.1
  132.2 302.0 %while.58 = (s32[]{:T(128)}, f32[1,768]{1,0:T(1,128)S(1)}, f32[1,768]{1,0:T(1,128)S(1)}, f32[32,1,32,768]{3,2,1,0:T(8,128)S(1)}, f32[32,1,768]{2,1,0:T(1,128)}, ...) while((s32[]{:T(128)}, f32[1,768]{1,0:T(1,128)S(1)}, ...), condition=%wide.region_8.9_spmd.clone.clone.clone.clone, body=%wide.region_4.8_spmd.clone.clone.clone.sunk.clone | while | flops 5907907 | bytes 1656024 | solution.py:102
  434.3 3.7 reshape.1478
  444.7 5.2 fusion.88
  457.5 8.2 reshape.1488
  465.7 10.0 fusion.114
  475.7 9.3 reshape.1489
  485.0 9.5 fusion.91
  494.6 4.0 fusion.66
  498.5 11.5 multiply_convert_fusion
  510.1 7.3 fusion.116
  517.5 8.0 convolution_bitcast_fusion
  525.5 12.6 fusion.90
  544.8 5.6 fusion.77
  558.6 3.6 fusion.71
  562.2 695.1 %while.59 = (s32[]{:T(128)}, f32[32,32,768]{2,1,0:T(8,128)}, f32[32,768]{1,0:T(8,128)}, f32[768]{0:T(1024)}, f32[32,768]{1,0:T(8,128)}, /*index=5*/f32[768]{0:T(...) while((s32[]{:T(128)}, f32[32,32,768]{2,1,0:T(8,128)}, ...), condition=%wide.region_18.19_spmd.clone.clone.clone.clone, body=%wide.region_13.18_spmd.clone.clone.clone.sunk.clone | while | flops 15496388 | bytes 48774152 | solution.py:102
  1257.3 4.7 fusion.120
  1262.1 3.7 reshape.1498
  1268.7 3.5 reshape.1500
  1272.2 4.3 fusion.96
  1282.9 9.5 copy.94
  1292.4 10.8 reshape.1505
  1306.4 3.4 reshape.1482
  1311.7 3.5 fusion.119
  1322.6 4.5 fusion.81
  1329.1 42.0 %all-reduce.4 = f32[11,768]{1,0:T(8,128)S(1)} all-reduce(f32[11,768]{1,0:T(8,128)S(1)} %stack.32), channel_id=2, replica_groups=mesh['wide'=16,'narrow'=2] {'wide','narrow'}, use_global_device_ids=true, to_apply=%region_38.39.clone | all-reduce | flops 8448 | bytes 67584
  1371.8 4.5 add_convert_fusion
  1376.3 399.4 %all-reduce.15.cloned.1.call-done = (f32[589824]{0:T(1024)}, f32[589824]{0:T(1024)}, f32[589824]{0:T(1024)}, f32[589824]{0:T(1024)}, f32[2359296]{0:T(1024)}, /*index=5*/f32[2359296]{0:T(1024)}, f32[589824]{0:T(1024)}) async-done(((f32[589824]{0:T(1024)}, f32[589824]{0:T(1024)}, f32[589824]{0:T(1024)}, f32[589824]{0:T(1024)}, f32[2359296]{0:T(1024)}, /*index=5*/f32[2359296]{0:T(1024)}, f32[589824]{0:T(1024)}), ...) | async-done | bytes 30670864
  (3081 shorter events, 1064.7 us)
Async XLA Ops:
  7.2 78.0 %copy-start.3 = (bf16[1,1024,768]{2,1,0:T(8,128)(2,1)S(1)}, bf16[1,1024,768]{2,1,0:T(8,128)(2,1)}, u32[]{:S(2)}) copy-start(bf16[1,1024,768]{2,1,0:T(8,128)(2,1)} %param.15) | copy-start | bytes 4718596
  7.2 87.7 %all-gather.11.cloned.1.call-start = ((), (), s32[]{:S(2)}) async-start(), calls=%async_computation.1 | async-start | bytes 1216512 | tf_op jit(solution)/shard_map/all_gather | solution.py:159
  7.9 115.9 %all-gather.13.cloned.1.call-start = ((), (), s32[]{:S(2)}) async-start(), calls=%async_computation.2 | async-start | bytes 1216512 | tf_op jit(solution)/shard_map/all_gather | solution.py:160
  8.7 425.6 %all-gather.9.cloned.1.call-start = ((), (), s32[]{:S(2)}) async-start(), calls=%async_computation | async-start | bytes 1216512 | tf_op jit(solution)/shard_map/all_gather | solution.py:158
  9.4 428.6 %all-gather.15.cloned.1.call-start = ((), (), s32[]{:S(2)}) async-start(), calls=%async_computation.3 | async-start | bytes 1216512 | tf_op jit(solution)/shard_map/all_gather | solution.py:161
  10.0 431.4 %all-gather.17.cloned.1.call-start = ((), (), s32[]{:S(2)}) async-start(), calls=%async_computation.4 | async-start | bytes 1216512 | tf_op jit(solution)/shard_map/all_gather | solution.py:164
  10.6 446.9 %all-gather.19.cloned.1.call-start = ((), (), s32[]{:S(2)}) async-start(), calls=%async_computation.5 | async-start | bytes 4866048 | tf_op jit(solution)/shard_map/all_gather | solution.py:162
  11.1 464.6 %all-gather.21.cloned.1.call-start = ((), (), s32[]{:S(2)}) async-start(), calls=%async_computation.6 | async-start | bytes 4866048 | tf_op jit(solution)/shard_map/all_gather | solution.py:163
  11.9 1763.8 %all-reduce.15.cloned.1.call-start = ((), (), s32[]{:S(2)}) async-start(), calls=%async_computation.7 | async-start | bytes 61341696
  12.3 82.6 %copy-start.17 = (bf16[32,1,32,768]{3,2,1,0:T(8,128)(2,1)}, bf16[32,1,32,768]{3,2,1,0:T(8,128)(2,1)S(1)}, u32[]{:S(2)}) copy-start(bf16[32,1,32,768]{3,2,1,0:T(8,128)(2,1)S(1)} %fusion.112) | copy-start | bytes 4718596
  13.9 529.3 %copy-start.43 = (f32[1024]{0:T(1024)}, f32[1024]{0:T(1024)S(1)}, u32[]{:S(2)}) copy-start(f32[1024]{0:T(1024)S(1)} %broadcast_subtract_fusion.1) | copy-start | bytes 12292
  434.2 10.5 copy-start.29
  485.0 9.6 copy-start.15
  485.0 9.6 copy-start.36
  485.0 9.6 copy-start.38
  494.6 15.5 slice-start
  498.5 11.5 slice-start.1
  510.1 7.4 copy-start.37
  510.1 7.4 copy-start.90
  517.5 8.0 copy-start.32
  525.5 12.6 copy-start.93
  573.0 7.2 copy-start
  594.7 7.2 copy-start
  616.5 7.2 copy-start
  638.2 7.2 copy-start
  659.9 7.2 copy-start
  681.6 7.2 copy-start
  703.3 7.2 copy-start
  725.1 7.2 copy-start
  746.8 7.2 copy-start
  1327.2 44.6 %copy-start.16 = (bf16[1,1024,768]{2,1,0:T(8,128)(2,1)S(1)}, bf16[1,1024,768]{2,1,0:T(8,128)(2,1)}, u32[]{:S(2)}) copy-start(bf16[1,1024,768]{2,1,0:T(8,128)(2,1)} %param.17) | copy-start | bytes 4718596
  1327.2 44.6 %copy-start.81 = (f32[1024]{0:T(1024)S(1)}, f32[1024]{0:T(1024)}, u32[]{:S(2)}) copy-start(f32[1024]{0:T(1024)} %copy-done.80) | copy-start | bytes 12292
  (754 other events, 2569.0 us)
Sparse Core Ops, SparseCore 0:
  10.9 56.8 all-gather.10
  70.8 53.0 all-gather.12
  126.8 53.1 all-gather.8
  182.7 53.0 all-gather.14
  238.5 53.2 all-gather.16
  294.6 62.5 all-gather.18
  360.1 62.4 all-gather.20
  1306.5 469.1 all-reduce.14
where the time goes:
time: 1810 us; the launch traced here: 1790 us
  other arithmetic  679 us (38%)
  local copies, waits for them, and re-layouts  437 us (24%)
  waiting for transfers between devices  426 us (24%)
  blocking collectives  113 us (6%)
  matrix products  108 us (6%)
    unnamed x9, waiting for transfers between devices  404 us
    squeeze x192, local copies, waits for them, and re-layouts, block_weighted_kv_sum(): lax.scan(jax.checkpoint(advance), (zero_state, zero_state), (arrange(addr...  205 us
    dot_general x96, other arithmetic, advance(): jnp.einsum('rijd,rjd->rid', pair, weight * tile_content_rows, precision=l...  124 us
    dynamic_update_slice x96, other arithmetic, block_weighted_kv_sum(): lax.scan(jax.checkpoint(advance), (zero_state, zero_state), (arrange(addr...  76.9 us
    all_gather x1, blocking collectives, per_device(): lax.all_gather(vectors, ('wide', 'narrow'), axis=1, tiled=True)  70.7 us
    slice x64, local copies, waits for them, and re-layouts, advance(): ending = jnp.where(segment == segment[:, -1:], 1.0, 0.0)  61.9 us
    mul x64, other arithmetic, advance(): factor = carried[:, -1:] * stretch  61.1 us
    another operation x64, other arithmetic, advance(): segment = jnp.cumsum(1.0 - continue_block, axis=-1)  49.3 us
  transfers between devices with their start and end apart: 8, of which 2 were waited for; matrix products, arithmetic and copies ran while one was open for 22% of the time, Pallas kernels for 0%

commit v1 on v0

v1 whole, which is shorter than its diff:
```python
from functools import partial

import jax
import jax.numpy as jnp
from jax import lax
from jax.experimental import pallas as pl
from jax.experimental.pallas import tpu as pltpu
from jax.sharding import PartitionSpec as P


SEG = 16
LANES = 128
EPS = 1e-05
F32 = jnp.float32
BF16 = jnp.bfloat16
VMEM_LIMIT = 62 * 1024 * 1024


def wide_of(column, width):
    return jnp.concatenate([column] * (width // LANES), axis=1)


def dot_nn(left, right):
    return jnp.dot(left, right, preferred_element_type=F32)


def dot_nt(left, right):
    return lax.dot_general(left, right, (((1,), (1,)), ((), ())), preferred_element_type=F32)


def dot_tn(left, right):
    return lax.dot_general(left, right, (((0,), (0,)), ((), ())), preferred_element_type=F32)


def local(source, target, sem):
    return pltpu.make_async_copy(source, target, sem)


def rows_at(index, size):
    return pl.ds(pl.multiple_of(index * size, size), size)


def fill_mask(lengths, mask, length):
    steps = length // SEG

    @pl.loop(0, length // 128)
    def _(block):
        row = block * 128 + lax.broadcasted_iota(jnp.int32, (128, LANES), 0)
        place = (row % SEG) * steps + row // SEG
        start = jnp.int32(0)
        fresh = place == 0
        for doc in range(lengths.shape[1] - 1):
            start = start + lengths[0, doc]
            fresh = jnp.logical_or(fresh, place == start)
        mask[rows_at(block, 128), :] = jnp.where(fresh, 0.0, 1.0)


def widen(source, target):
    @pl.loop(0, source.shape[0] // 32)
    def _(block):
        rows = rows_at(block, 32)
        for c in range(target.shape[0]):
            target[c, rows, :] = source[rows, c * LANES : (c + 1) * LANES].astype(F32)


def narrow(source, target):
    @pl.loop(0, target.shape[0] // 32)
    def _(block):
        rows = rows_at(block, 32)
        for c in range(source.shape[0]):
            target[rows, c * LANES : (c + 1) * LANES] = source[c, rows, :].astype(BF16)


def take_step(source, step, steps):
    strip = pl.ds(step, SEG, stride=steps)
    return jnp.concatenate([source[c, strip, :] for c in range(source.shape[0])], axis=1)


def put_step(target, step, steps, rows):
    strip = pl.ds(step, SEG, stride=steps)
    for c in range(target.shape[0]):
        target[c, strip, :] = rows[:, c * LANES : (c + 1) * LANES]


def norm_rows(rows):
    centred = rows - jnp.mean(rows, axis=-1, keepdims=True)
    scale = lax.rsqrt(jnp.mean(centred * centred, axis=-1, keepdims=True) + EPS)
    return centred * scale, scale


def join_runs(local_end, through, backward):
    index = lax.broadcasted_iota(jnp.int32, local_end[0].shape, 0)
    if backward:
        index = SEG - 1 - index
    states = list(local_end)
    hop = 1
    while hop < SEG:
        turn = SEG - hop if backward else hop
        inside = index >= hop
        moved = pltpu.roll(through, turn, 0)
        states = [jnp.where(inside, s + through * pltpu.roll(s, turn, 0), s) for s in states]
        through = jnp.where(inside, through * moved, through)
        hop *= 2
    turn = SEG - 1 if backward else 1
    return [jnp.where(index >= 1, pltpu.roll(s, turn, 0), 0.0) for s in states]


def forward_kernel(
    lengths, tokens, cotangent, vec, w4_in, wk_in, wv_in, wg_in,
    result, n1_out, n2_out, r_out, mix_out, state_out, att_out, cig_out, sq_out, gsg_out, up_out,
    w4, wk, wv, wg, nat, norm, mid, state, half, sq, mask, rsd, sems,
):
    length, width = tokens.shape
    steps = length // SEG

    load_tok = local(tokens, half.at[0], sems.at[0])
    load_cot = local(cotangent, half.at[1], sems.at[1])
    load_w4 = local(w4_in, w4, sems.at[2])
    load_wk = local(wk_in, wk, sems.at[3])
    load_wv = local(wv_in, wv, sems.at[4])
    load_wg = local(wg_in, wg, sems.at[5])
    for copy in (load_tok, load_cot, load_w4, load_wk, load_wv, load_wg):
        copy.start()
    fill_mask(lengths, mask, length)
    load_tok.wait()
    widen(half.at[0], nat)

    @pl.loop(0, steps, unroll=2)
    def _(step):
        rows = take_step(nat, step, steps)
        mid[rows_at(step, SEG), :] = rows
        normed, scale = norm_rows(rows)
        norm[rows_at(step + 1, SEG), :] = normed
        rsd[0, rows_at(step, SEG), :] = jnp.broadcast_to(scale, (SEG, LANES))

    norm[0:SEG, :] = pltpu.roll(norm[length : length + SEG, :], 1, 0)
    save_n1 = local(norm, n1_out, sems.at[6])
    save_n1.start()

    @pl.loop(0, steps, unroll=2)
    def _(step):
        gain, bias = vec[0:1, :], vec[1:2, :]
        rows = rows_at(step, SEG)
        now = norm[rows_at(step + 1, SEG), :] * gain + bias
        before = (norm[rows, :] * gain + bias) * wide_of(mask[rows, :], width)
        change = now - before
        for q in range(3):
            half[2 + q, rows, :] = (before + vec[2 + q : 3 + q, :] * change).astype(BF16)

    save_mix = local(half.at[2:5], mix_out, sems.at[7])
    save_mix.start()

    load_w4.wait()
    for q in range(3):

        @pl.loop(0, 2)
        def _(part):
            rows = rows_at(part, length // 2)
            pre = dot_nn(half[2 + q, rows, :], w4[:, q].reshape(width, width))
            if q == 0:
                pre = jax.nn.sigmoid(pre)
            if q == 1:
                pre = jnp.exp(pre)
            state[q, rows, :] = pre

    rate = -jnp.exp(vec[5:6, :])
    fade = jnp.exp(rate)

    def first(step, carry):
        top, bottom, through = carry
        rows = rows_at(step, SEG)
        keep = mask[rows, :]
        factor = fade * wide_of(keep, width)
        key = state[1, rows, :]
        return factor * top + key * state[2, rows, :], factor * bottom + key, through * keep

    zero = jnp.zeros((SEG, width), F32)
    top, bottom, through = lax.fori_loop(0, steps, first, (zero, zero, jnp.ones((SEG, LANES), F32)), unroll=2)
    through = wide_of(through, width) * jnp.exp(rate * steps)
    top, bottom = join_runs((top, bottom), through, False)

    def second(step, carry):
        top, bottom = carry
        rows = rows_at(step, SEG)
        keep = wide_of(mask[rows, :], width)
        top, bottom = top * keep, bottom * keep
        key = state[1, rows, :]
        key_value = key * state[2, rows, :]
        bonus = jnp.exp(vec[6:7, :])
        blended = (top + bonus * key_value) / (bottom + bonus * key)
        half[5, rows, :] = (state[0, rows, :] * blended).astype(BF16)
        state[3, rows, :] = top
        state[4, rows, :] = bottom
        return fade * top + key_value, fade * bottom + key

    lax.fori_loop(0, steps, second, (top, bottom), unroll=2)
    save_state = local(state, state_out, sems.at[8])
    save_state.start()
    save_att = local(half.at[5], att_out, sems.at[9])
    save_att.start()

    @pl.loop(0, 2)
    def _(part):
        rows = rows_at(part, length // 2)
        mid[rows, :] += dot_nn(half[5, rows, :], w4[:, 3].reshape(width, width))

    save_n1.wait()

    @pl.loop(0, steps, unroll=2)
    def _(step):
        rows = rows_at(step, SEG)
        normed, scale = norm_rows(mid[rows, :])
        norm[rows_at(step + 1, SEG), :] = normed
        rsd[1, rows, :] = jnp.broadcast_to(scale, (SEG, LANES))

    norm[0:SEG, :] = pltpu.roll(norm[length : length + SEG, :], 1, 0)
    save_n2 = local(norm, n2_out, sems.at[10])
    save_n2.start()
    save_r = local(rsd, r_out, sems.at[11])
    save_r.start()
    save_mix.wait()

    @pl.loop(0, steps, unroll=2)
    def _(step):
        gain, bias = vec[7:8, :], vec[8:9, :]
        rows = rows_at(step, SEG)
        now = norm[rows_at(step + 1, SEG), :] * gain + bias
        before = (norm[rows, :] * gain + bias) * wide_of(mask[rows, :], width)
        change = now - before
        for q in range(2):
            half[2 + q, rows, :] = (before + vec[9 + q : 10 + q, :] * change).astype(BF16)

    save_cig = local(half.at[2:4], cig_out, sems.at[12])
    save_cig.start()

    load_cot.wait()
    widen(half.at[1], nat)

    @pl.loop(0, steps, unroll=2)
    def _(step):
        half[0, rows_at(step, SEG), :] = take_step(nat, step, steps).astype(BF16)

    save_up = local(half.at[0], up_out, sems.at[13])
    save_up.start()

    load_wk.wait()
    for q in range(4):

        @pl.loop(0, 2)
        def _(part):
            rows = rows_at(part, length // 2)
            pre = jnp.maximum(dot_nn(half[2, rows, :], wk[:, q].reshape(width, width)), 0.0)
            sq[rows, q * width : (q + 1) * width] = (pre * pre).astype(BF16)

    save_sq = local(sq, sq_out, sems.at[14])
    save_sq.start()

    save_state.wait()
    load_wg.wait()
    load_wv.wait()

    @pl.loop(0, 2)
    def _(part):
        rows = rows_at(part, length // 2)
        state[0, rows, :] = jax.nn.sigmoid(dot_nn(half[3, rows, :], wg[...].reshape(width, width)))
        state[1, rows, :] = dot_nn(sq[rows, :], wv[...].reshape(4 * width, width))

    save_att.wait()

    @pl.loop(0, steps, unroll=2)
    def _(step):
        rows = rows_at(step, SEG)
        gate, shrunk = state[0, rows, :], state[1, rows, :]
        upstream = half[0, rows, :].astype(F32)
        gated = gate * shrunk
        put_step(nat, step, steps, mid[rows, :] + gated)
        half[4, rows, :] = (upstream * gate).astype(BF16)
        half[5, rows, :] = (upstream * gated * (1.0 - gate)).astype(BF16)

    save_gsg = local(half.at[4:6], gsg_out, sems.at[15])
    save_gsg.start()
    narrow(nat, half.at[1])
    save_res = local(half.at[1], result, sems.at[16])
    save_res.start()
    for copy in (save_n2, save_r, save_cig, save_up, save_sq, save_gsg, save_res):
        copy.wait()


def backward_kernel(
    lengths, vec, w4_in, wk_in, wv_in, wg_in, n1_in, n2_in, r_in, mix_in, state_in, att_in, cig_in, sq_in, gsg_in, up_in,
    input_grad, vec_grad, g4_out, gk_out, gv_out, gg_out,
    wk, wv, wg, big, sq, half, mask, rsd, nat, grad, grad_gate, sums, sems,
):
    length, width = input_grad.shape
    steps = length // SEG
    n_buf, gm_buf, nb_buf, s_buf = 0, 1, 2, 3

    load_gsg = local(gsg_in, half.at[0:2], sems.at[0])
    load_sq = local(sq_in, sq, sems.at[1])
    load_wv = local(wv_in, wv, sems.at[2])
    load_cig = local(cig_in, half.at[2:4], sems.at[3])
    load_wk = local(wk_in, wk, sems.at[4])
    load_wg = local(wg_in, wg, sems.at[5])
    load_n2 = local(n2_in, big.at[n_buf], sems.at[6])
    load_r = local(r_in, rsd, sems.at[7])
    for copy in (load_gsg, load_sq, load_wv, load_cig, load_wk, load_wg, load_n2, load_r):
        copy.start()
    fill_mask(lengths, mask, length)

    load_gsg.wait()
    load_sq.wait()

    @pl.loop(0, 4)
    def _(part):
        out = dot_tn(sq[:, rows_at(part, width)], half[0]).astype(BF16)
        grad[pl.ds(part * 4, 4)] = out.reshape(4, 4, 48, width)

    save_gv = local(grad, gv_out, sems.at[8])
    save_gv.start()

    load_wv.wait()

    @pl.loop(0, 4)
    def _(part):
        cols = rows_at(part, width)
        back = dot_nt(half[0], wv[pl.ds(part * 4, 4)].reshape(width, width))
        expanded = jnp.sqrt(sq[:, cols].astype(F32))
        sq[:, cols] = (2.0 * expanded * back).astype(BF16)

    load_mix = local(mix_in, wv.reshape(3, length, width), sems.at[9])
    load_mix.start()

    load_cig.wait()
    grad_gate[...] = dot_tn(half[3], half[1]).astype(BF16).reshape(16, 48, width)
    save_gg = local(grad_gate, gg_out, sems.at[10])
    save_gg.start()

    load_wg.wait()
    load_wk.wait()
    big[s_buf, 0:length, :] = dot_nt(half[1], wg[...].reshape(width, width))
    load_up = local(up_in, half.at[1], sems.at[11])
    load_up.start()

    @pl.loop(0, 2)
    def _(part):
        rows = rows_at(part, length // 2)
        out = dot_nt(sq[rows, 0:width], wk[:, 0].reshape(width, width))
        for q in range(1, 4):
            out += dot_nt(sq[rows, q * width : (q + 1) * width], wk[:, q].reshape(width, width))
        big[gm_buf, rows, :] = out

    load_w4 = local(w4_in, wk, sems.at[12])
    load_w4.start()

    save_gv.wait()
    for q in range(4):
        grad[:, q] = dot_tn(half[2], sq[:, q * width : (q + 1) * width]).astype(BF16).reshape(16, 48, width)
    save_gk = local(grad, gk_out, sems.at[13])
    save_gk.start()
    load_att = local(att_in, sq.at[:, 0:width], sems.at[14])
    load_att.start()

    load_n2.wait()
    load_r.wait()

    zero8 = jnp.zeros((8, width), F32)
    zero = jnp.zeros((SEG, width), F32)

    def fold(rows):
        return rows[0:8] + rows[8:16]

    def mix_two(step, carry):
        sum_channel, sum_gate = carry
        rows = rows_at(step, SEG)
        gain, bias = vec[7:8, :], vec[8:9, :]
        keep = wide_of(mask[rows, :], width)
        now = big[n_buf, rows_at(step + 1, SEG), :] * gain + bias
        before = (big[n_buf, rows, :] * gain + bias) * keep
        change = now - before
        in_channel, in_gate = big[gm_buf, rows, :], big[s_buf, rows, :]
        mix_channel, mix_gate = vec[9:10, :], vec[10:11, :]
        scaled = mix_channel * in_channel + mix_gate * in_gate
        big[gm_buf, rows, :] = scaled
        big[nb_buf, rows, :] = (in_channel + in_gate - scaled) * keep
        return sum_channel + fold(in_channel * change), sum_gate + fold(in_gate * change)

    sum_channel, sum_gate = lax.fori_loop(0, steps, mix_two, (zero8, zero8), unroll=2)
    sums[9:10, :] = jnp.sum(sum_channel, axis=0, keepdims=True)
    sums[10:11, :] = jnp.sum(sum_gate, axis=0, keepdims=True)
    big[nb_buf, length : length + SEG, :] = pltpu.roll(big[nb_buf, 0:SEG, :], SEG - 1, 0)
    load_up.wait()

    def norm_two(step, carry):
        sum_gain, sum_bias = carry
        rows = rows_at(step, SEG)
        normed = big[n_buf, rows_at(step + 1, SEG), :]
        incoming = big[gm_buf, rows, :] + big[nb_buf, rows_at(step + 1, SEG), :]
        scaled = incoming * vec[7:8, :]
        mean = jnp.mean(scaled, axis=-1, keepdims=True)
        along = jnp.mean(scaled * normed, axis=-1, keepdims=True)
        scale = wide_of(rsd[1, rows, :], width)
        out = half[1, rows, :].astype(F32) + scale * (scaled - mean - normed * along)
        big[gm_buf, rows, :] = out
        half[0, rows, :] = out.astype(BF16)
        return sum_gain + fold(incoming * normed), sum_bias + fold(incoming)

    sum_gain, sum_bias = lax.fori_loop(0, steps, norm_two, (zero8, zero8), unroll=2)
    sums[7:8, :] = jnp.sum(sum_gain, axis=0, keepdims=True)
    sums[8:9, :] = jnp.sum(sum_bias, axis=0, keepdims=True)
    load_n1 = local(n1_in, big.at[n_buf], sems.at[15])
    load_n1.start()
    load_state = local(state_in, big.at[3:8, 0:length], sems.at[16])
    load_state.start()

    load_att.wait()
    load_w4.wait()
    save_gk.wait()
    grad[:, 3] = dot_tn(sq[:, 0:width], half[0]).astype(BF16).reshape(16, 48, width)

    @pl.loop(0, 2)
    def _(part):
        rows = rows_at(part, length // 2)
        big[nb_buf, rows, :] = dot_nt(half[0, rows, :], wk[:, 3].reshape(width, width))

    rate = -jnp.exp(vec[5:6, :])
    fade = jnp.exp(rate)
    load_state.wait()

    def first(index, carry):
        right, below, through = carry
        step = steps - 1 - index
        rows = rows_at(step, SEG)
        keep_column = mask[rows, :]
        keep = wide_of(keep_column, width)
        bonus = jnp.exp(vec[6:7, :])
        gate, key, value = big[s_buf, rows, :], big[s_buf + 1, rows, :], big[s_buf + 2, rows, :]
        own = bonus * key
        inverse = 1.0 / (big[s_buf + 4, rows, :] + own)
        blended = (big[s_buf + 3, rows, :] + own * value) * inverse
        incoming = big[nb_buf, rows, :] * gate
        sq[rows, width : 2 * width] = (incoming * blended * (1.0 - gate)).astype(BF16)
        weight = incoming * inverse
        big[nb_buf, rows, :] = weight
        big[s_buf, rows, :] = blended
        right = keep * (weight + fade * right)
        below = keep * (weight * blended + fade * below)
        return right, below, through * keep_column

    right, below, through = lax.fori_loop(0, steps, first, (zero, zero, jnp.ones((SEG, LANES), F32)), unroll=2)
    through = wide_of(through, width) * jnp.exp(rate * steps)
    right, below = join_runs((right, below), through, True)

    def second(index, carry):
        right, below, sum_decay, sum_bonus = carry
        step = steps - 1 - index
        rows = rows_at(step, SEG)
        keep = wide_of(mask[rows, :], width)
        bonus = jnp.exp(vec[6:7, :])
        weight, blended = big[nb_buf, rows, :], big[s_buf, rows, :]
        key, value = big[s_buf + 1, rows, :], big[s_buf + 2, rows, :]
        own = bonus * key * weight
        own_key = own * (value - blended)
        sq[rows, 2 * width : 3 * width] = (own_key + key * (right * value - below)).astype(BF16)
        sq[rows, 3 * width : 4 * width] = (own + key * right).astype(BF16)
        sum_bonus = sum_bonus + fold(own_key)
        sum_decay = sum_decay + fold(right * big[s_buf + 3, rows, :] - below * big[s_buf + 4, rows, :])
        right = keep * (weight + fade * right)
        below = keep * (weight * blended + fade * below)
        return right, below, sum_decay, sum_bonus

    _, _, sum_decay, sum_bonus = lax.fori_loop(0, steps, second, (right, below, zero8, zero8), unroll=2)
    sums[5:6, :] = jnp.sum(sum_decay, axis=0, keepdims=True) * (rate * fade)
    sums[6:7, :] = jnp.sum(sum_bonus, axis=0, keepdims=True)

    load_mix.wait()
    mixed = wv.reshape(3, length, width)
    for q in range(3):
        grad[:, q] = dot_tn(mixed[q], sq[:, (q + 1) * width : (q + 2) * width]).astype(BF16).reshape(16, 48, width)
    save_g4 = local(grad, g4_out, sems.at[17])
    save_g4.start()
    for q, place in enumerate((s_buf, s_buf + 3, s_buf + 4)):

        @pl.loop(0, 2)
        def _(part):
            rows = rows_at(part, length // 2)
            big[place, rows, :] = dot_nt(
                sq[rows, (q + 1) * width : (q + 2) * width], wk[:, q].reshape(width, width)
            )

    load_n1.wait()

    def mix_one(step, carry):
        rows = rows_at(step, SEG)
        gain, bias = vec[0:1, :], vec[1:2, :]
        keep = wide_of(mask[rows, :], width)
        now = big[n_buf, rows_at(step + 1, SEG), :] * gain + bias
        before = (big[n_buf, rows, :] * gain + bias) * keep
        change = now - before
        out = []
        scaled, total = None, None
        for q, place in enumerate((s_buf, s_buf + 3, s_buf + 4)):
            incoming = big[place, rows, :]
            part = vec[2 + q : 3 + q, :] * incoming
            scaled = part if scaled is None else scaled + part
            total = incoming if total is None else total + incoming
            out.append(carry[q] + fold(incoming * change))
        big[s_buf, rows, :] = scaled
        big[nb_buf, rows, :] = (total - scaled) * keep
        return tuple(out)

    sum_mix = lax.fori_loop(0, steps, mix_one, (zero8, zero8, zero8), unroll=2)
    for q in range(3):
        sums[2 + q : 3 + q, :] = jnp.sum(sum_mix[q], axis=0, keepdims=True)
    big[nb_buf, length : length + SEG, :] = pltpu.roll(big[nb_buf, 0:SEG, :], SEG - 1, 0)

    def norm_one(step, carry):
        sum_gain, sum_bias = carry
        rows = rows_at(step, SEG)
        normed = big[n_buf, rows_at(step + 1, SEG), :]
        incoming = big[s_buf, rows, :] + big[nb_buf, rows_at(step + 1, SEG), :]
        scaled = incoming * vec[0:1, :]
        mean = jnp.mean(scaled, axis=-1, keepdims=True)
        along = jnp.mean(scaled * normed, axis=-1, keepdims=True)
        scale = wide_of(rsd[0, rows, :], width)
        out = big[gm_buf, rows, :] + scale * (scaled - mean - normed * along)
        put_step(nat, step, steps, out)
        return sum_gain + fold(incoming * normed), sum_bias + fold(incoming)

    sum_gain, sum_bias = lax.fori_loop(0, steps, norm_one, (zero8, zero8), unroll=2)
    sums[0:1, :] = jnp.sum(sum_gain, axis=0, keepdims=True)
    sums[1:2, :] = jnp.sum(sum_bias, axis=0, keepdims=True)
    sums[11:16, :] = jnp.zeros((5, width), F32)
    narrow(nat, half.at[0])
    save_in = local(half.at[0], input_grad, sems.at[18])
    save_in.start()
    save_vec = local(sums, vec_grad, sems.at[19])
    save_vec.start()
    for copy in (save_gg, save_g4, save_in, save_vec):
        copy.wait()


ANY = pl.BlockSpec(memory_space=pl.ANY)
SMEM = pl.BlockSpec(memory_space=pltpu.SMEM)
VMEM = pl.BlockSpec(memory_space=pltpu.VMEM)


def run_forward(lengths, tokens, cotangent, vec, w4, wk, wv, wg):
    length, width = tokens.shape
    shape = jax.ShapeDtypeStruct
    outs = (
        shape((length, width), BF16),
        shape((length + SEG, width), F32),
        shape((length + SEG, width), F32),
        shape((2, length, LANES), F32),
        shape((3, length, width), BF16),
        shape((5, length, width), F32),
        shape((length, width), BF16),
        shape((2, length, width), BF16),
        shape((length, 4 * width), BF16),
        shape((2, length, width), BF16),
        shape((length, width), BF16),
    )
    return pl.pallas_call(
        forward_kernel,
        out_shape=outs,
        in_specs=[SMEM, ANY, ANY, VMEM, ANY, ANY, ANY, ANY],
        out_specs=[ANY] * len(outs),
        scratch_shapes=[
            pltpu.VMEM((16, 4, 48, width), BF16),
            pltpu.VMEM((16, 4, 48, width), BF16),
            pltpu.VMEM((16, 192, width), BF16),
            pltpu.VMEM((16, 48, width), BF16),
            pltpu.VMEM((width // LANES, length, LANES), F32),
            pltpu.VMEM((length + SEG, width), F32),
            pltpu.VMEM((length, width), F32),
            pltpu.VMEM((5, length, width), F32),
            pltpu.VMEM((6, length, width), BF16),
            pltpu.VMEM((length, 4 * width), BF16),
            pltpu.VMEM((length, LANES), F32),
            pltpu.VMEM((2, length, LANES), F32),
            pltpu.SemaphoreType.DMA((17,)),
        ],
        compiler_params=pltpu.CompilerParams(vmem_limit_bytes=VMEM_LIMIT),
        name="forward",
    )(lengths, tokens, cotangent, vec, w4, wk, wv, wg)


def run_backward(lengths, vec, w4, wk, wv, wg, saved):
    n1, n2, r, mix, state, att, cig, sq, gsg, up = saved
    length, width = up.shape
    shape = jax.ShapeDtypeStruct
    slabs = shape((16, 4, 48, width), BF16)
    outs = (shape((length, width), BF16), shape((16, width), F32), slabs, slabs, slabs, shape((16, 48, width), BF16))
    return pl.pallas_call(
        backward_kernel,
        out_shape=outs,
        in_specs=[SMEM, VMEM] + [ANY] * 14,
        out_specs=[ANY] * len(outs),
        scratch_shapes=[
            pltpu.VMEM((16, 4, 48, width), BF16),
            pltpu.VMEM((16, 192, width), BF16),
            pltpu.VMEM((16, 48, width), BF16),
            pltpu.VMEM((8, length + SEG, width), F32),
            pltpu.VMEM((length, 4 * width), BF16),
            pltpu.VMEM((4, length, width), BF16),
            pltpu.VMEM((length, LANES), F32),
            pltpu.VMEM((2, length, LANES), F32),
            pltpu.VMEM((width // LANES, length, LANES), F32),
            pltpu.VMEM((16, 4, 48, width), BF16),
            pltpu.VMEM((16, 48, width), BF16),
            pltpu.VMEM((16, width), F32),
            pltpu.SemaphoreType.DMA((20,)),
        ],
        compiler_params=pltpu.CompilerParams(vmem_limit_bytes=VMEM_LIMIT),
        name="backward",
    )(lengths, vec, w4, wk, wv, wg, n1, n2, r, mix, state, att, cig, sq, gsg, up)


AXES = ("wide", "narrow")


def per_device(
    tokens, lengths, cotangent, vectors,
    time_recept, time_key, time_value, time_output, channel_key, channel_value, channel_recept,
):
    _, length, width = tokens.shape

    def whole(part, axis=0):
        return lax.all_gather(part, AXES, axis=axis, tiled=True)

    vec = jnp.pad(whole(vectors, 1).astype(F32), ((0, 5), (0, 0)))
    square = [whole(m).reshape(16, 48, width) for m in (time_recept, time_key, time_value, time_output)]
    w4 = jnp.stack(square, axis=1)
    wk = jnp.swapaxes(whole(channel_key).reshape(16, 48, 4, width), 1, 2)
    wv = whole(channel_value).reshape(16, 192, width)
    wg = whole(channel_recept).reshape(16, 48, width)
    out = run_forward(lengths, tokens[0], cotangent[0], vec, w4, wk, wv, wg)
    input_grad, vec_grad, g4, gk, gv, gg = run_backward(lengths, vec, w4, wk, wv, wg, out[1:])

    def owned(full, axis=0):
        return lax.psum_scatter(full.astype(F32), AXES, scatter_dimension=axis, tiled=True)

    return (
        out[0][None],
        input_grad[None],
        owned(vec_grad[:11], 1),
        *[owned(g4[:, q].reshape(-1)) for q in range(4)],
        owned(jnp.swapaxes(gk, 1, 2).reshape(-1)),
        owned(gv.reshape(-1)),
        owned(gg.reshape(-1)),
    )


def solution(mesh):
    both = P(AXES)
    rows = P(AXES, None, None)
    return jax.shard_map(
        per_device,
        mesh=mesh,
        in_specs=(rows, P(AXES, None), rows, P(None, AXES)) + (both,) * 7,
        out_specs=(rows, rows, P(None, AXES)) + (both,) * 7,
        check_vma=False,
    )
```

time: 1810 us -> 1120 us (0.62)
  other arithmetic: 679 us -> 13.6 us
  local copies, waits for them, and re-layouts: 437 us -> 105 us
  waiting for transfers between devices: 426 us -> 736 us
  Pallas kernels: 0 us -> 124 us
  matrix products: 108 us -> 0 us
    all_gather x7, waiting for transfers between devices: 22 us -> 305 us  [whole(): return lax.all_gather(part, AXES, axis=axis, tiled=True)]
    squeeze x192 -> x0, local copies, waits for them, and re-layouts: 205 us -> none  [block_weighted_kv_sum(): lax.scan(jax.checkpoint(advance), (zero_state, zero_state), (arrange(addr...]
    dot_general x96 -> x0, other arithmetic: 124 us -> none  [advance(): jnp.einsum('rijd,rjd->rid', pair, weight * tile_content_rows, precision=l...]
    pallas_call x0 -> x2, Pallas kernels: none -> 124 us  [the longest x1 72.9 us: run_backward(): pl.pallas_call(backward_kernel, out_shape=outs, in_specs=[SMEM, VMEM] + [...]
    dot_general x21 -> x0, matrix products: 108 us -> none  [the longest x7 39.7 us: multiply(): return jnp.dot(left_in, right_in, preferred_element_type=jnp.float32)]
    slice x128 -> x0, local copies, waits for them, and re-layouts: 99.3 us -> none  [the longest x64 61.9 us: advance(): ending = jnp.where(segment == segment[:, -1:], 1.0, 0.0)]
    mul x99 -> x0, other arithmetic: 83.8 us -> none  [the longest x64 61.1 us: advance(): factor = carried[:, -1:] * stretch]
    select_n x128 -> x0, other arithmetic: 78.7 us -> none  [the longest x96 40.6 us: advance(): carried = jnp.where(segment == 0.0, 1.0, 0.0)]
  transfers between devices with their start and end apart: 8 -> 8, of which waited for: 2 -> 7; matrix products, arithmetic and copies ran while one was open for 22% -> 3% of each run, Pallas kernels for 0% -> 0%
where the time goes in v1:
time: 1120 us; the launch traced here: 1110 us
  waiting for transfers between devices  736 us (66%)
  Pallas kernels  124 us (11%)
  blocking collectives  113 us (10%)
  local copies, waits for them, and re-layouts  105 us (9%)
  between operations  14.7 us (1%)
  other arithmetic  13.6 us (1%)
    unnamed x9, waiting for transfers between devices  430 us
    all_gather x7, waiting for transfers between devices, whole(): return lax.all_gather(part, AXES, axis=axis, tiled=True)  305 us
    pallas_call x1, Pallas kernels, run_backward(): pl.pallas_call(backward_kernel, out_shape=outs, in_specs=[SMEM, VMEM] + [...  72.9 us
    all_gather x1, blocking collectives, whole(): return lax.all_gather(part, AXES, axis=axis, tiled=True)  70.7 us
    pallas_call x1, Pallas kernels, run_forward(): pl.pallas_call(forward_kernel, out_shape=outs, in_specs=[SMEM, ANY, ANY,...  51 us
    convert_element_type x8, local copies, waits for them, and re-layouts, owned(): full.astype(F32)  49.6 us
    unnamed x1, blocking collectives  42 us
  transfers between devices with their start and end apart: 8, of which 7 were waited for; matrix products, arithmetic and copies ran while one was open for 3% of the time, Pallas kernels for 0%

profile of v1, /device:TPU:0, one launch (start us, length us, event | category | flops | bytes accessed | tf_op | source)
XLA Modules:
  0.0 1105.9 jit_solution(3907856073793835300)
XLA Ops:
  11.9 70.7 %all-gather = bf16[32,24,11]{1,2,0:T(8,128)(2,1)S(1)} all-gather(bf16[1,24,11]{1,2,0:T(8,128)(2,1)} %bitcast.34), channel_id=1, replica_groups=mesh['wide'=16,'narrow'=2] {'wide','narrow'}, dimensions={0}, use_global_device_ids=true | all-gather | bytes 17424 | tf_op jit(solution)/shard_map/all_gather | solution.py:629
  83.5 2.6 stack_reshape.12
  86.1 37.8 %all-gather.11.cloned.1.call-done = bf16[589824]{0:T(1024)(128)(2,1)} async-done(((bf16[18432]{0:T(1024)(128)(2,1)}), bf16[589824]{0:T(1024)(128)(2,1)}) %all-gather.11.cloned.1.call-update) | async-done | bytes 1179664 | tf_op jit(solution)/shard_map/all_gather | solution.py:629
  123.9 2.6 stack_reshape.13
  126.4 53.5 %all-gather.13.cloned.1.call-done = bf16[589824]{0:T(1024)(128)(2,1)} async-done(((bf16[18432]{0:T(1024)(128)(2,1)}), bf16[589824]{0:T(1024)(128)(2,1)}) %all-gather.13.cloned.1.call-update) | async-done | bytes 1179664 | tf_op jit(solution)/shard_map/all_gather | solution.py:629
  179.9 2.6 stack_reshape.14
  182.5 53.3 %all-gather.15.cloned.1.call-done = bf16[589824]{0:T(1024)(128)(2,1)} async-done(((bf16[18432]{0:T(1024)(128)(2,1)}), bf16[589824]{0:T(1024)(128)(2,1)}) %all-gather.15.cloned.1.call-update) | async-done | bytes 1179664 | tf_op jit(solution)/shard_map/all_gather | solution.py:629
  235.8 3.3 stack_reshape.15
  239.1 52.5 %all-gather.21.cloned.1.call-done = bf16[589824]{0:T(1024)(128)(2,1)} async-done(((bf16[18432]{0:T(1024)(128)(2,1)}), bf16[589824]{0:T(1024)(128)(2,1)}) %all-gather.21.cloned.1.call-update) | async-done | bytes 1179664 | tf_op jit(solution)/shard_map/all_gather | solution.py:629
  291.7 3.3 reshape.48.wg_in
  299.5 57.6 %all-gather.17.cloned.1.call-done = bf16[2359296]{0:T(1024)(128)(2,1)} async-done(((bf16[73728]{0:T(1024)(128)(2,1)}), bf16[2359296]{0:T(1024)(128)(2,1)}) %all-gather.17.cloned.1.call-update) | async-done | bytes 4718608 | tf_op jit(solution)/shard_map/all_gather | solution.py:629
  357.0 9.3 reshape.46
  366.4 5.4 copy.31
  371.8 50.6 %all-gather.19.cloned.1.call-done = bf16[2359296]{0:T(1024)(128)(2,1)} async-done(((bf16[73728]{0:T(1024)(128)(2,1)}), bf16[2359296]{0:T(1024)(128)(2,1)}) %all-gather.19.cloned.1.call-update) | async-done | bytes 4718608 | tf_op jit(solution)/shard_map/all_gather | solution.py:629
  422.4 9.2 reshape.47.wv_in
  431.7 51.0 %forward.1 = (bf16[1024,768]{1,0:T(8,128)(2,1)}, f32[1040,768]{1,0:T(8,128)}, f32[1040,768]{1,0:T(8,128)}, f32[2,1024,128]{2,1,0:T(8,128)}, bf16[3,1024,768]{2,1...) custom-call(s32[1,4]{1,0:T(1,128)} %lengths.3, ...), custom_call_target="tpu_custom_call" | custom-call | tf_op jit(solution)/shard_map/forward/pallas_call | solution.py:563
  482.7 72.9 %backward.1 = (bf16[1024,768]{1,0:T(8,128)(2,1)}, f32[16,768]{1,0:T(8,128)}, bf16[16,4,48,768]{3,2,1,0:T(8,128)(2,1)}, bf16[16,4,48,768]{3,2,1,0:T(8,128)(2,1)},...) custom-call(s32[1,4]{1,0:T(1,128)} %lengths.3, f32[16,768]{1,0:T(8,128)} %pad_convert_fusion.vec, ...), custom_call_target="tpu_custom_call" | custom-call | tf_op jit(solution)/shard_map/backward/pallas_call | solution.py:594
  555.6 5.6 slice_convert_fusion
  561.2 3.2 reshape.49
  564.5 3.2 reshape.50
  567.7 3.2 reshape.51
  570.9 1.6 reshape.52
  572.5 7.3 convert_bitcast_fusion
  579.8 13.5 %copy.27 = f32[16,48,4,768]{3,2,1,0:T(4,128)} copy(f32[16,48,4,768]{3,1,2,0:T(8,128)} %convert_bitcast_fusion) | data formatting | bytes 18874368 | tf_op jit(solution)/shard_map/convert_element_type | solution.py:641
  593.4 12.4 %reshape.53 = f32[2359296]{0:T(1024)} reshape(f32[16,48,4,768]{3,2,1,0:T(4,128)} %copy.27) | data formatting | bytes 18874368 | tf_op jit(solution)/shard_map/convert_element_type | solution.py:641
  605.8 10.1 reshape.54
  615.8 2.4 reshape.55
  619.0 42.0 %all-reduce.1 = f32[11,768]{1,0:T(8,128)S(1)} all-reduce(f32[11,768]{1,0:T(8,128)S(1)} %bitcast.33), channel_id=2, replica_groups=mesh['wide'=16,'narrow'=2] {'wide','narrow'}, use_global_device_ids=true, to_apply=%region_0.1.clone | all-reduce | flops 8448 | bytes 67584
  661.7 426.0 %all-reduce.12.cloned.1.call-done = (f32[589824]{0:T(1024)}, f32[589824]{0:T(1024)}, f32[589824]{0:T(1024)}, f32[589824]{0:T(1024)}, f32[2359296]{0:T(1024)}, /*index=5*/f32[2359296]{0:T(1024)}, f32[589824]{0:T(1024)}) async-done(((f32[589824]{0:T(1024)}, f32[589824]{0:T(1024)}, f32[589824]{0:T(1024)}, f32[589824]{0:T(1024)}, f32[2359296]{0:T(1024)}, /*index=5*/f32[2359296]{0:T(1024)}, f32[589824]{0:T(1024)}), ...) | async-done | bytes 30670864
  1087.7 1.5 dynamic-slice.1
  1093.8 1.7 dynamic-slice.5
  1095.4 1.7 dynamic-slice.6
  (35 shorter events, 17.5 us)
Async XLA Ops:
  7.2 76.3 %all-gather.9.cloned.1.call-start = ((), (), s32[]{:S(2)}) async-start(), calls=%async_computation | async-start | bytes 1216512 | tf_op jit(solution)/shard_map/all_gather | solution.py:629
  7.9 116.0 %all-gather.11.cloned.1.call-start = ((), (), s32[]{:S(2)}) async-start(), calls=%async_computation.1 | async-start | bytes 1216512 | tf_op jit(solution)/shard_map/all_gather | solution.py:629
  8.7 171.2 %all-gather.13.cloned.1.call-start = ((), (), s32[]{:S(2)}) async-start(), calls=%async_computation.2 | async-start | bytes 1216512 | tf_op jit(solution)/shard_map/all_gather | solution.py:629
  9.4 226.4 %all-gather.15.cloned.1.call-start = ((), (), s32[]{:S(2)}) async-start(), calls=%async_computation.3 | async-start | bytes 1216512 | tf_op jit(solution)/shard_map/all_gather | solution.py:629
  10.0 281.7 %all-gather.21.cloned.1.call-start = ((), (), s32[]{:S(2)}) async-start(), calls=%async_computation.6 | async-start | bytes 1216512 | tf_op jit(solution)/shard_map/all_gather | solution.py:629
  10.6 346.5 %all-gather.17.cloned.1.call-start = ((), (), s32[]{:S(2)}) async-start(), calls=%async_computation.4 | async-start | bytes 4866048 | tf_op jit(solution)/shard_map/all_gather | solution.py:629
  11.1 411.3 %all-gather.19.cloned.1.call-start = ((), (), s32[]{:S(2)}) async-start(), calls=%async_computation.5 | async-start | bytes 4866048 | tf_op jit(solution)/shard_map/all_gather | solution.py:629
  11.9 1075.8 %all-reduce.12.cloned.1.call-start = ((), (), s32[]{:S(2)}) async-start(), calls=%async_computation.7 | async-start | bytes 61341696
  296.2 2.2 copy-start
  605.8 10.1 copy-start.1
  618.2 0.8 copy-start.2
Sparse Core Ops, SparseCore 0:
  10.9 56.8 all-gather.8
  70.7 53.0 all-gather.10
  126.8 53.0 all-gather.12
  182.7 53.0 all-gather.14
  238.5 53.0 all-gather.20
  294.4 62.5 all-gather.16
  360.0 62.4 all-gather.18
  618.3 469.2 all-reduce.11
